TPU v7x, 32 devices: a whole 2x2x4 slice. The times are simulated.
32 devices in a mesh: dp: 16 (over z, y, core), seq: 2 (over x).
Axes of the slice: x: 2, y: 2, z: 4, core: 2. Of those that a mesh axis runs over, the one named last changes fastest.
Arguments:
- tokens: bfloat16 [256, 4096], P('seq', 'dp'), may hold values from -6 to 6
- in_weight: bfloat16 [2, 4096, 8192], P(None, 'seq', 'dp'), may hold values from -0.09375 to 0.09375
- conv_weight: bfloat16 [4, 8192], P(None, 'dp'), may hold values from -0.5 to 0.5
- conv_bias: bfloat16 [8192], P('dp'), may hold values from -1 to 1
- out_weight: bfloat16 [8192, 4096], P('dp', 'seq'), may hold values from -0.0625 to 0.0625
- grad_out: bfloat16 [256, 4096], P('seq', 'dp'), may hold values from -6 to 6
Outputs:
- output: bfloat16 [256, 4096], P('seq', 'dp')
- grad_tokens: bfloat16 [256, 4096], P('seq', 'dp')
- grad_in_weight: float32 [2, 4096, 8192], P(None, 'seq', 'dp')
- grad_out_weight: float32 [8192, 4096], P('dp', 'seq')
- grad_conv_weight: float32 [4, 8192], P(None, 'dp')
- grad_conv_bias: float32 [8192], P('dp')
All inputs are finite; a program needn't handle non-finite values.
Results may differ from a plain program's by a relative error of at most 0.012.
Values may be sent and summed in bfloat16 or wider, within the bound.
A program may use at most 128 MiB of HBM per device.

v0:
```python
import jax
import jax.numpy as jnp
from jax import lax
from jax.sharding import PartitionSpec as P


def from_behind(block, axis, distance):
    devices = range(lax.axis_size(axis))
    route = [(i - distance, i) for i in devices if i - distance in devices]
    return lax.ppermute(block, axis, route)


def silu_parts(value):
    sig = jax.nn.sigmoid(value)
    return (value * sig, sig * (1.0 + value * (1.0 - sig)))


def on_device(tokens, in_weight, conv_weight, conv_bias, out_weight, grad_out):
    in_full, out_full = (
        lax.all_gather(in_weight, "seq", axis=1, tiled=True),
        lax.all_gather(out_weight, "seq", axis=1, tiled=True),
    )
    whole = lax.all_gather(tokens, "dp", axis=1, tiled=True)
    tok_rows = whole.shape[0]
    taps = conv_weight.shape[0]
    mixed = jnp.einsum("td,pde->tpe", whole, in_full, preferred_element_type=jnp.float32).astype(
        jnp.bfloat16
    )
    inner = mixed[:, 0, :]
    gate_in = mixed[:, 1, :]
    rim = from_behind(inner[tok_rows - (taps - 1) :], "seq", 1)
    padded = jnp.concatenate([rim, inner], axis=0)
    conv = jnp.broadcast_to(conv_bias.astype(jnp.float32)[None, :], inner.shape)
    for lag in range(taps):
        conv = conv + conv_weight[lag].astype(jnp.float32)[None, :] * padded[
            lag : lag + tok_rows
        ].astype(jnp.float32)
    act, act_slope = silu_parts(conv)
    gate, gate_slope = silu_parts(gate_in.astype(jnp.float32))
    hidden = (act * gate).astype(jnp.bfloat16)
    columns = lax.all_to_all(out_full, "dp", split_axis=1, concat_axis=0, tiled=True)
    output = jnp.dot(
        lax.all_gather(hidden, "dp", axis=1, tiled=True),
        columns,
        preferred_element_type=jnp.float32,
    ).astype(jnp.bfloat16)
    upstream = lax.all_gather(grad_out, "dp", axis=1, tiled=True)
    back = lax.dot_general(
        upstream, out_full, (((1,), (1,)), ((), ())), preferred_element_type=jnp.float32
    )
    grad_conv = (back * gate * act_slope).astype(jnp.bfloat16)
    grad_gate = (back * act * gate_slope).astype(jnp.bfloat16)
    ahead_rim = from_behind(grad_conv[: taps - 1], "seq", -1)
    ahead = jnp.concatenate([grad_conv, ahead_rim], axis=0)
    grad_inner = jnp.zeros(inner.shape, jnp.float32)
    for lag in range(taps):
        shift_start = taps - 1 - lag
        grad_inner = grad_inner + conv_weight[lag].astype(jnp.float32)[None, :] * ahead[
            shift_start : shift_start + tok_rows
        ].astype(jnp.float32)
    grad_inner = grad_inner.astype(jnp.bfloat16)
    conv_float = grad_conv.astype(jnp.float32)
    tap_rows = []
    for lag in range(taps):
        tap_rows.append(
            jnp.sum(conv_float * padded[lag : lag + tok_rows].astype(jnp.float32), axis=0)
        )
    tap_grads, bias_grads = lax.psum(
        (jnp.stack(tap_rows, axis=0), jnp.sum(conv_float, axis=0)), "seq"
    )
    branch_grads = jnp.stack([grad_inner, grad_gate], axis=1)
    term_in = jnp.einsum("td,tpe->pde", whole, branch_grads, preferred_element_type=jnp.float32)
    term_out = lax.dot_general(
        hidden, upstream, (((0,), (0,)), ((), ())), preferred_element_type=jnp.float32
    )
    grad_in_weight, grad_out_weight = (
        lax.psum_scatter(
            term_in.astype(jnp.bfloat16), "seq", scatter_dimension=1, tiled=True
        ).astype(jnp.float32),
        lax.psum_scatter(
            term_out.astype(jnp.bfloat16), "seq", scatter_dimension=1, tiled=True
        ).astype(jnp.float32),
    )
    feature_rows = lax.all_to_all(in_full, "dp", split_axis=1, concat_axis=2, tiled=True)
    grad_tokens = jnp.einsum(
        "tpe,pde->td",
        lax.all_gather(branch_grads, "dp", axis=2, tiled=True),
        feature_rows,
        preferred_element_type=jnp.float32,
    )
    grad_tokens = grad_tokens.astype(jnp.bfloat16)
    return (output, grad_tokens, grad_in_weight, grad_out_weight, tap_grads, bias_grads)


def solution(mesh):
    return jax.shard_map(
        on_device,
        mesh=mesh,
        in_specs=(
            P("seq", "dp"),
            P(None, "seq", "dp"),
            P(None, "dp"),
            P("dp"),
            P("dp", "seq"),
            P("seq", "dp"),
        ),
        out_specs=(
            P("seq", "dp"),
            P("seq", "dp"),
            P(None, "seq", "dp"),
            P("dp", "seq"),
            P(None, "dp"),
            P("dp"),
        ),
        check_vma=False,
    )
```

profile of v0, /device:TPU:3, one launch (start us, length us, event | category | flops | bytes accessed | tf_op | source)
XLA Modules:
  0.0 668.1 jit_solution(906129579470852858)
XLA Ops:
  7.2 0.0 all-gather.7.cloned.1.call-start
  7.2 0.7 all-gather.7.cloned.1.call-update
  7.9 0.0 all-gather.9.cloned.1.call-start
  8.0 0.7 all-gather.9.cloned.1.call-update
  8.7 0.0 copy-start.4
  8.7 0.0 all-gather.15.cloned.1.call-start
  8.7 0.7 all-gather.15.cloned.1.call-update
  9.4 0.0 all-gather.13.cloned.1.call-start
  9.5 2.5 copy.23
  12.0 0.0 all-gather.13.cloned.1.call-update
  12.0 0.0 all-gather.11.cloned.1.call-start
  12.1 36.5 %all-gather.7.cloned.1.call-done = bf16[128,4096]{1,0:T(8,128)(2,1)} async-done(((bf16[128,256]{1,0:T(8,128)(2,1)}), bf16[128,4096]{1,0:T(8,128)(2,1)}) %all-gather.7.cloned.1.call-update) | async-done | bytes 1048592 | tf_op jit(solution)/shard_map/all_gather | solution.py:23
  48.6 103.8 %all-gather.9.cloned.1.call-done = bf16[2,4096,512]{2,1,0:T(8,128)(2,1)} async-done(((bf16[2,2048,512]{2,1,0:T(8,128)(2,1)}), bf16[2,4096,512]{2,1,0:T(8,128)(2,1)}) %all-gather.9.cloned.1.call-update) | async-done | bytes 8388624 | tf_op jit(solution)/shard_map/all_gather | solution.py:20
  152.3 5.0 convolution_convert_fusion.1
  157.3 1.3 collective-permute-start
  158.6 34.0 %all-gather.15.cloned.1.call-done = bf16[128,4096]{1,0:T(8,128)(2,1)} async-done(((bf16[128,256]{1,0:T(8,128)(2,1)}), bf16[128,4096]{1,0:T(8,128)(2,1)}) %all-gather.15.cloned.1.call-update) | async-done | bytes 1048592 | tf_op jit(solution)/shard_map/all_gather | solution.py:47
  192.6 56.9 %all-gather.13.cloned.1.call-done = bf16[512,4096]{0,1:T(8,128)(2,1)} async-done(((bf16[512,2048]{0,1:T(8,128)(2,1)}), bf16[512,4096]{0,1:T(8,128)(2,1)}) %all-gather.13.cloned.1.call-update) | async-done | bytes 4194320 | tf_op jit(solution)/shard_map/all_gather | solution.py:21
  249.6 0.0 collective-permute-done
  249.6 3.6 convert_reduce_fusion
  253.2 0.8 fusion.25
  254.0 0.0 all-gather.11.cloned.1.call-update
  254.1 0.0 reduce-scatter.5.cloned.1.call-start
  254.1 4.1 convolution_convert_fusion
  258.3 0.0 reduce-scatter.5.cloned.1.call-update
  258.3 0.0 all-gather.17.cloned.1.call-start
  258.4 3.2 collective-permute-start.1
  261.5 0.7 collective-permute-done.1
  262.3 0.1 fusion.26
  262.4 0.7 pad_maximum_fusion
  263.1 0.0 all-gather.17.cloned.1.call-update
  263.2 7.2 %all-to-all-start = ((bf16[512,16,256]{0,2,1:T(8,128)(2,1)}), bf16[512,16,256]{0,2,1:T(8,128)(2,1)}, u32[]{:S(2)}, u32[]{:S(2)}) async-start(bf16[512,16,256]{0,2,1:T(8,128)(2,1)} %bitcast.61), calls=%async_computation | async-start | bytes 8388608 | tf_op jit(solution)/shard_map/all_to_all | solution.py:41
  270.4 0.0 reduce-scatter.3.cloned.1.call-start
  270.4 5.6 convert_bitcast_fusion
  276.0 0.0 reduce-scatter.3.cloned.1.call-update
  276.0 16.4 %copy.25 = bf16[2,4096,512]{2,0,1:T(2,128)(2,1)} copy(bf16[2,4096,512]{2,1,0:T(8,128)(2,1)} %all-gather.9.cloned.1.call-done) | data formatting | bytes 16777216 | tf_op jit(solution)/shard_map/all_gather | solution.py:20
  292.4 65.1 %all-to-all-done = bf16[512,16,256]{0,2,1:T(8,128)(2,1)} async-done(((bf16[512,16,256]{0,2,1:T(8,128)(2,1)}), bf16[512,16,256]{0,2,1:T(8,128)(2,1)}, u32[]{:S(2)}, u32[]{:S(2)}) %all-to-all-start) | async-done | bytes 4194336 | tf_op jit(solution)/shard_map/all_to_all | solution.py:41
  357.5 20.0 %all-to-all-start.1 = ((bf16[2,4096,512]{2,0,1:T(2,128)(2,1)}), bf16[2,4096,512]{2,0,1:T(2,128)(2,1)}, u32[]{:S(2)}, u32[]{:S(2)}) async-start(bf16[2,4096,512]{2,0,1:T(2,128)(2,1)} %copy.25), calls=%async_computation.1 | async-start | bytes 16777216 | tf_op jit(solution)/shard_map/all_to_all | solution.py:84
  377.5 8.0 %all-reduce = (f32[4,512]{1,0:T(4,128)}, f32[512]{0:T(512)}) all-reduce(f32[4,512]{1,0:T(4,128)S(1)} %pad_maximum_fusion.3, f32[512]{0:T(512)S(1)} %get-tuple-element.33), channel_id=1, replica_groups=mesh['dp'=16,'seq'=2] {'seq'}, use_global_device_ids=true, to_apply=%region_6.0 | all-reduce | flops 2560 | bytes 20480 | tf_op jit(solution)/shard_map/psum | solution.py:68
  385.5 6.4 copy.24
  391.9 4.2 convolution_convert_fusion.2
  396.1 11.8 %reduce-scatter.5.cloned.1.call-done = bf16[512,2048]{1,0:T(8,128)(2,1)} async-done(((bf16[512,4096]{1,0:T(8,128)(2,1)}), bf16[512,2048]{1,0:T(8,128)(2,1)}) %reduce-scatter.5.cloned.1.call-update) | async-done | bytes 2097168 | tf_op jit(solution)/shard_map/reduce_scatter | solution.py:80
  407.9 4.1 convert_element_type.108
  412.0 142.0 %all-to-all-done.1 = bf16[2,4096,512]{2,0,1:T(2,128)(2,1)} async-done(((bf16[2,4096,512]{2,0,1:T(2,128)(2,1)}), bf16[2,4096,512]{2,0,1:T(2,128)(2,1)}, u32[]{:S(2)}, u32[]{:S(2)}) %all-to-all-start.1) | async-done | bytes 8388640 | tf_op jit(solution)/shard_map/all_to_all | solution.py:84
  554.0 11.5 %copy.31 = bf16[2,16,256,512]{3,1,2,0:T(8,128)(2,1)} copy(bf16[2,16,256,512]{3,0,2,1:T(2,128)(2,1)} %bitcast.14) | data formatting | bytes 16777216 | tf_op jit(solution)/shard_map/all_to_all | solution.py:84
  565.5 13.6 %all_to_all.34 = bf16[2,256,8192]{2,1,0:T(8,128)(2,1)} reshape(bf16[2,256,16,512]{3,2,1,0:T(8,128)(2,1)} %bitcast.59) | data formatting | bytes 16777216 | tf_op jit(solution)/shard_map/all_to_all | solution.py:84
  579.1 8.5 %fusion = bf16[128,256]{1,0:T(8,128)(2,1)} fusion(bf16[128,2,8192]{2,0,1:T(8,128)(2,1)} %all-gather.17.cloned.1.call-done, bf16[2,256,8192]{2,1,0:T(8,128)(2,1)} %all_to_all.34), kind=kOutput, calls=%fused_computation.6 | convolution fusion | flops 1073774592 | bytes 12648448 | tf_op jit(solution)/shard_map/tpe,pde->td/dot_general | solution.py:85
  587.6 66.8 %reduce-scatter.3.cloned.1.call-done = bf16[2,2048,512]{1,2,0:T(8,128)(2,1)} async-done(((bf16[2,4096,512]{1,2,0:T(8,128)(2,1)}), bf16[2,2048,512]{1,2,0:T(8,128)(2,1)}) %reduce-scatter.3.cloned.1.call-update) | async-done | bytes 4194320 | tf_op jit(solution)/shard_map/reduce_scatter | solution.py:77
  654.4 6.9 %copy.28 = f32[2,2048,512]{2,1,0:T(8,128)} copy(bf16[2,2048,512]{1,2,0:T(8,128)(2,1)} %reduce-scatter.3.cloned.1.call-done) | data formatting | bytes 12582912
  (17 shorter events, 0.1 us)
Async XLA Ops:
  7.2 2.3 copy-start.1
  7.2 41.4 %all-gather.7.cloned.1.call-start = ((), (), s32[]{:S(2)}) async-start(), calls=%async_computation.4 | async-start | bytes 1114112 | tf_op jit(solution)/shard_map/all_gather | solution.py:23
  7.9 144.4 %all-gather.9.cloned.1.call-start = ((), (), s32[]{:S(2)}) async-start(), calls=%async_computation.5 | async-start | bytes 12582912 | tf_op jit(solution)/shard_map/all_gather | solution.py:20
  8.7 3.4 copy-start.4
  8.7 3.4 copy-start.3
  8.7 184.0 %all-gather.15.cloned.1.call-start = ((), (), s32[]{:S(2)}) async-start(), calls=%async_computation.8 | async-start | bytes 1114112 | tf_op jit(solution)/shard_map/all_gather | solution.py:47
  9.4 240.2 %all-gather.13.cloned.1.call-start = ((), (), s32[]{:S(2)}) async-start(), calls=%async_computation.7 | async-start | bytes 6291456 | tf_op jit(solution)/shard_map/all_gather | solution.py:21
  12.0 379.9 %all-gather.11.cloned.1.call-start = ((), (), s32[]{:S(2)}) async-start(), calls=%async_computation.6 | async-start | bytes 2228224 | tf_op jit(solution)/shard_map/all_gather | solution.py:43
  157.3 92.3 %collective-permute-start = (bf16[3,512]{1,0:T(4,128)(2,1)S(1)}, bf16[3,512]{1,0:T(4,128)(2,1)S(1)}, u32[]{:S(2)}, u32[]{:S(2)}) collective-permute-start(bf16[3,512]{1,0:T(4,128)(2,1)S(1)} %slice_bitcast_fusion.2), channel_id=1, source_target_pairs={{0,1},{2,3},{4,5},{6,7},{8,9},{10,11},{12,13},{14,15},{16,17},{18,... | collective-permute-start | bytes 9224 | tf_op jit(solution)/shard_map/ppermute | solution.py:10
  249.6 4.5 copy-start.2
  254.1 153.8 %reduce-scatter.5.cloned.1.call-start = ((), (), s32[]{:S(2)}) async-start(), calls=%async_computation.11 | async-start | bytes 6291456 | tf_op jit(solution)/shard_map/reduce_scatter | solution.py:80
  258.3 320.8 %all-gather.17.cloned.1.call-start = ((), (), s32[]{:S(2)}) async-start(), calls=%async_computation.9 | async-start | bytes 4456448 | tf_op jit(solution)/shard_map/all_gather | solution.py:87
  258.4 3.9 collective-permute-start.1
  263.2 7.2 %copy-start = (bf16[128,4096]{1,0:T(8,128)(2,1)S(1)}, bf16[128,4096]{1,0:T(8,128)(2,1)}, u32[]{:S(2)}) copy-start(bf16[128,4096]{1,0:T(8,128)(2,1)} %all-gather.7.cloned.1.call-done) | copy-start | bytes 3145732
  263.2 94.3 %all-to-all-start = ((bf16[512,16,256]{0,2,1:T(8,128)(2,1)}), bf16[512,16,256]{0,2,1:T(8,128)(2,1)}, u32[]{:S(2)}, u32[]{:S(2)}) async-start(bf16[512,16,256]{0,2,1:T(8,128)(2,1)} %bitcast.61), calls=%async_computation | async-start | bytes 8388608 | tf_op jit(solution)/shard_map/all_to_all | solution.py:41
  270.4 384.0 %reduce-scatter.3.cloned.1.call-start = ((), (), s32[]{:S(2)}) async-start(), calls=%async_computation.10 | async-start | bytes 12582912 | tf_op jit(solution)/shard_map/reduce_scatter | solution.py:77
  357.5 196.5 %all-to-all-start.1 = ((bf16[2,4096,512]{2,0,1:T(2,128)(2,1)}), bf16[2,4096,512]{2,0,1:T(2,128)(2,1)}, u32[]{:S(2)}, u32[]{:S(2)}) async-start(bf16[2,4096,512]{2,0,1:T(2,128)(2,1)} %copy.25), calls=%async_computation.1 | async-start | bytes 16777216 | tf_op jit(solution)/shard_map/all_to_all | solution.py:84
Sparse Core Ops, SparseCore 0:
  10.2 38.3 all-gather.6
  50.1 102.1 all-gather.8
  154.5 38.1 all-gather.14
  194.6 54.9 all-gather.12
  254.2 91.1 all-gather.10
  347.6 60.2 reduce-scatter.4
  410.2 142.3 all-gather.16
  555.0 99.3 reduce-scatter.2
where the time goes:
time: 672 us; the launch traced here: 668 us
  waiting for transfers between devices  520 us (77%)
  local copies, waits for them, and re-layouts  57.3 us (9%)
  starting transfers between devices  32 us (5%)
  matrix products  31 us (5%)
  between operations  14.3 us (2%)
  blocking collectives  8 us (1%)
    all_to_all x1, waiting for transfers between devices, on_device(): lax.all_to_all(in_full, 'dp', split_axis=1, concat_axis=2, tiled=True)  142 us
    all_gather x1, waiting for transfers between devices, on_device(): lax.all_gather(in_weight, 'seq', axis=1, tiled=True)  104 us
    reduce_scatter x1, waiting for transfers between devices, on_device(): lax.psum_scatter(term_in.astype(jnp.bfloat16), 'seq', scatter_dimension=1...  66.8 us
    all_to_all x1, waiting for transfers between devices, on_device(): lax.all_to_all(out_full, 'dp', split_axis=1, concat_axis=0, tiled=True)  65.1 us
    all_gather x1, waiting for transfers between devices, on_device(): lax.all_gather(out_weight, 'seq', axis=1, tiled=True)  56.9 us
    all_gather x1, waiting for transfers between devices, on_device(): whole = lax.all_gather(tokens, 'dp', axis=1, tiled=True)  36.5 us
    all_gather x1, waiting for transfers between devices, on_device(): upstream = lax.all_gather(grad_out, 'dp', axis=1, tiled=True)  34 us
    all_to_all x2, local copies, waits for them, and re-layouts, on_device(): lax.all_to_all(in_full, 'dp', split_axis=1, concat_axis=2, tiled=True)  25.1 us
  transfers between devices with their start and end apart: 12, of which 9 were waited for; matrix products, arithmetic and copies ran while one was open for 10% of the time, Pallas kernels for 0%

commit v1 on v0

v1 whole, which is shorter than its diff:
```python
import jax
import jax.numpy as jnp
from jax import lax
from jax.sharding import PartitionSpec as P


def silu_parts(value):
    sig = jax.nn.sigmoid(value)
    return (value * sig, sig * (1.0 + value * (1.0 - sig)))


def routes():
    n, m = lax.axis_size("dp"), lax.axis_size("seq")
    per = n // m
    there = [
        (j * m + t, (t * per + j % per) * m + j // per) for j in range(n) for t in range(m)
    ]
    return there, [(b, a) for a, b in there]


def on_device(tokens, in_weight, conv_weight, conv_bias, out_weight, grad_out):
    n, m = lax.axis_size("dp"), lax.axis_size("seq")
    per = n // m
    rows, cols = tokens.shape
    total = rows * m
    width = per * cols
    taps, chans = conv_weight.shape
    there, back_route = routes()

    both = jnp.stack([tokens, grad_out])
    moved = lax.ppermute(both, ("dp", "seq"), there)
    gathered = lax.all_gather(moved, "dp")
    arranged = gathered.reshape(m, per, 2, rows, cols).transpose(2, 0, 3, 1, 4)
    arranged = arranged.reshape(2, total, width)
    whole, upstream = arranged[0], arranged[1]

    mixed = jnp.einsum("td,pde->pte", whole, in_weight, preferred_element_type=jnp.float32)
    back_part = lax.dot_general(
        upstream, out_weight, (((1,), (1,)), ((), ())), preferred_element_type=jnp.float32
    )
    parts = jnp.concatenate(
        [mixed.astype(jnp.bfloat16), back_part.astype(jnp.bfloat16)[None]], axis=0
    )
    parts = lax.all_gather(parts, "seq").astype(jnp.float32)
    sums = parts[0]
    for i in range(1, m):
        sums = sums + parts[i]
    inner = sums[0].astype(jnp.bfloat16).astype(jnp.float32)
    gate_in = sums[1].astype(jnp.bfloat16).astype(jnp.float32)
    back = sums[2]

    zeros = jnp.zeros((taps - 1, chans), jnp.float32)
    padded = jnp.concatenate([zeros, inner], axis=0)
    taps_f = conv_weight.astype(jnp.float32)
    conv = jnp.broadcast_to(conv_bias.astype(jnp.float32)[None, :], inner.shape)
    for lag in range(taps):
        conv = conv + taps_f[lag][None, :] * padded[lag : lag + total]
    act, act_slope = silu_parts(conv)
    gate, gate_slope = silu_parts(gate_in)
    hidden = (act * gate).astype(jnp.bfloat16)
    grad_conv = (back * gate * act_slope).astype(jnp.bfloat16).astype(jnp.float32)
    grad_gate = (back * act * gate_slope).astype(jnp.bfloat16)
    ahead = jnp.concatenate([grad_conv, zeros], axis=0)
    grad_inner = jnp.zeros(inner.shape, jnp.float32)
    for lag in range(taps):
        start = taps - 1 - lag
        grad_inner = grad_inner + taps_f[lag][None, :] * ahead[start : start + total]
    grad_inner = grad_inner.astype(jnp.bfloat16)
    tap_grads = jnp.stack(
        [jnp.sum(grad_conv * padded[lag : lag + total], axis=0) for lag in range(taps)], axis=0
    )
    bias_grads = jnp.sum(grad_conv, axis=0)

    out_part = jnp.dot(hidden, out_weight, preferred_element_type=jnp.float32)
    contract = (((1,), (1,)), ((), ()))
    tok_part = lax.dot_general(
        grad_inner, in_weight[0], contract, preferred_element_type=jnp.float32
    ) + lax.dot_general(grad_gate, in_weight[1], contract, preferred_element_type=jnp.float32)
    sent = jnp.stack([out_part.astype(jnp.bfloat16), tok_part.astype(jnp.bfloat16)])
    sent = sent.reshape(2, m, rows, per, cols).transpose(1, 3, 0, 2, 4)
    sent = sent.reshape(n, 2, rows, cols)
    summed = lax.psum_scatter(sent, "dp", scatter_dimension=0, tiled=False)
    result = lax.ppermute(summed, ("dp", "seq"), back_route)

    branch = jnp.stack([grad_inner, grad_gate])
    grad_in_weight = jnp.einsum(
        "td,pte->pde", whole, branch, preferred_element_type=jnp.float32
    )
    grad_out_weight = lax.dot_general(
        hidden, upstream, (((0,), (0,)), ((), ())), preferred_element_type=jnp.float32
    )
    return (result[0], result[1], grad_in_weight, grad_out_weight, tap_grads, bias_grads)


def solution(mesh):
    return jax.shard_map(
        on_device,
        mesh=mesh,
        in_specs=(
            P("seq", "dp"),
            P(None, "seq", "dp"),
            P(None, "dp"),
            P("dp"),
            P("dp", "seq"),
            P("seq", "dp"),
        ),
        out_specs=(
            P("seq", "dp"),
            P("seq", "dp"),
            P(None, "seq", "dp"),
            P("dp", "seq"),
            P(None, "dp"),
            P("dp"),
        ),
        check_vma=False,
    )
```

time: 672 us -> 203 us (0.30)
  waiting for transfers between devices: 520 us -> 130 us
  local copies, waits for them, and re-layouts: 57.3 us -> 23 us
  starting transfers between devices: 32 us -> 6.91 us
  matrix products: 31 us -> 17.9 us
  blocking collectives: 8 us -> 0 us
    all_to_all x2 -> x0, waiting for transfers between devices: 207 us -> none  [the longest x1 142 us: on_device(): lax.all_to_all(in_full, 'dp', split_axis=1, concat_axis=2, tiled=True)]
    all_gather x6 -> x2, waiting for transfers between devices: 231 us -> 67.6 us  [the longest x1 43 us: on_device(): gathered = lax.all_gather(moved, 'dp')]
    all_to_all x3 -> x0, local copies, waits for them, and re-layouts: 31.5 us -> none  [the longest x2 25.1 us: on_device(): lax.all_to_all(in_full, 'dp', split_axis=1, concat_axis=2, tiled=True)]
    all_to_all x2 -> x0, starting transfers between devices: 27.2 us -> none  [the longest x1 20 us: on_device(): lax.all_to_all(in_full, 'dp', split_axis=1, concat_axis=2, tiled=True)]
    reduce_scatter x2 -> x1, waiting for transfers between devices: 78.5 us -> 55.5 us  [on_device(): summed = lax.psum_scatter(sent, 'dp', scatter_dimension=0, tiled=False)]
    all_gather x1, local copies, waits for them, and re-layouts: 16.4 us -> 2.57 us  [on_device(): parts = lax.all_gather(parts, 'seq').astype(jnp.float32)]
    dot_general x5 -> x6, matrix products: 26.8 us -> 13.6 us  [the longest x1 5.71 us: on_device(): jnp.einsum('td,pte->pde', whole, branch, preferred_element_type=jnp.float32)]
    psum x1 -> x0, blocking collectives: 8 us -> none  [on_device(): lax.psum((jnp.stack(tap_rows, axis=0), jnp.sum(conv_float, axis=0)), 'seq')]
  transfers between devices with their start and end apart: 12 -> 5, of which waited for: 9 -> 4; matrix products, arithmetic and copies ran while one was open for 10% -> 10% of each run, Pallas kernels for 0% -> 0%
where the time goes in v1:
time: 203 us; the launch traced here: 200 us
  waiting for transfers between devices  130 us (64%)
  local copies, waits for them, and re-layouts  23 us (11%)
  matrix products  17.9 us (9%)
  between operations  13.9 us (7%)
  other arithmetic  8.23 us (4%)
  starting transfers between devices  6.91 us (3%)
    reduce_scatter x1, waiting for transfers between devices, on_device(): summed = lax.psum_scatter(sent, 'dp', scatter_dimension=0, tiled=False)  55.5 us
    all_gather x1, waiting for transfers between devices, on_device(): gathered = lax.all_gather(moved, 'dp')  43 us
    all_gather x1, waiting for transfers between devices, on_device(): parts = lax.all_gather(parts, 'seq').astype(jnp.float32)  24.6 us
    unnamed x18, local copies, waits for them, and re-layouts  11.7 us
    ppermute x1, waiting for transfers between devices, on_device(): moved = lax.ppermute(both, ('dp', 'seq'), there)  6.69 us
    dot_general x1, matrix products, on_device(): jnp.einsum('td,pte->pde', whole, branch, preferred_element_type=jnp.float32)  5.71 us
    dot_general x1, matrix products, on_device(): lax.dot_general(hidden, upstream, (((0,), (0,)), ((), ())), preferred_ele...  4.26 us
    ppermute x1, starting transfers between devices, on_device(): moved = lax.ppermute(both, ('dp', 'seq'), there)  4.19 us
  transfers between devices with their start and end apart: 5, of which 4 were waited for; matrix products, arithmetic and copies ran while one was open for 10% of the time, Pallas kernels for 0%

profile of v1, /device:TPU:3, one launch (start us, length us, event | category | flops | bytes accessed | tf_op | source)
XLA Modules:
  0.0 199.7 jit_solution(889629300262430790)
XLA Ops:
  7.2 0.0 copy-start
  7.2 0.0 all-gather.5.cloned.1.call-start
  7.2 1.0 pad_maximum_fusion.1
  8.3 4.2 %collective-permute-start = (bf16[2,128,256]{2,1,0:T(8,128)(2,1)S(1)}, bf16[2,128,256]{2,1,0:T(8,128)(2,1)S(1)}, u32[]{:S(2)}, u32[]{:S(2)}) collective-permute-start(bf16[2,128,256]{2,1,0:T(8,128)(2,1)S(1)} %pad_maximum_fusion.1), channel_id=1, source_target_pairs={{0,0},{1,16},{2,2},{3,18},{4,4},{5,20},{6,6},{7,22},{8,8},{9,24},{... | collective-permute-start | bytes 393224 | tf_op jit(solution)/shard_map/ppermute | solution.py:31
  12.5 6.7 %collective-permute-done = bf16[2,128,256]{2,1,0:T(8,128)(2,1)S(1)} collective-permute-done((bf16[2,128,256]{2,1,0:T(8,128)(2,1)S(1)}, bf16[2,128,256]{2,1,0:T(8,128)(2,1)S(1)}, u32[]{:S(2)}, u32[]{:S(2)}) %collective-permute-start) | collective-permute-done | bytes 131104 | tf_op jit(solution)/shard_map/ppermute | solution.py:31
  19.1 0.7 copy-done.4
  19.8 0.0 all-gather.5.cloned.1.call-update
  19.8 0.0 all-gather.7.cloned.1.call-start
  19.9 43.0 %all-gather.5.cloned.1.call-done = bf16[32,128,256]{2,1,0:T(8,128)(2,1)} async-done(((bf16[2,128,256]{2,1,0:T(8,128)(2,1)}), bf16[32,128,256]{2,1,0:T(8,128)(2,1)}) %all-gather.5.cloned.1.call-update) | async-done | bytes 2097168 | tf_op jit(solution)/shard_map/all_gather | solution.py:32
  62.8 2.8 %copy.24 = bf16[2,8,2,128,256]{4,1,3,0,2:T(8,128)(2,1)S(1)} copy(bf16[2,8,2,128,256]{4,3,2,1,0:T(8,128)(2,1)} %bitcast.95) | data formatting | bytes 4194304 | tf_op jit(solution)/shard_map/reshape | solution.py:33
  65.6 1.1 fusion.36
  66.7 1.3 copy.20
  68.0 2.4 %reshape.57 = bf16[256,2048,1]{1,0,2:T(8,128)(2,1)} reshape(bf16[1,2,128,8,256]{4,3,2,1,0:T(8,128)(2,1)} %get-tuple-element.27) | data formatting | bytes 2097152 | tf_op jit(solution)/shard_map/squeeze | solution.py:35
  70.4 0.0 copy-done
  70.4 2.1 %fusion.8 = bf16[1,256,512]{2,1,0:T(8,128)(2,1)S(1)} fusion(bf16[256,2048]{1,0:T(8,128)(2,1)} %bitcast.96, bf16[512,2048]{1,0:T(8,128)(2,1)S(1)} %copy-done), kind=kOutput, calls=%fused_computation.16 | convolution fusion | flops 537001984 | bytes 3407872 | tf_op jit(solution)/shard_map/dot_general | solution.py:38
  72.4 0.0 copy-done.1
  72.5 3.4 %fusion.7 = bf16[2,256,512]{2,1,0:T(8,128)(2,1)S(1)} fusion(bf16[256,2048,1]{1,0,2:T(8,128)(2,1)S(1)} %copy-done.1, bf16[2,2048,512]{2,1,0:T(8,128)(2,1)} %param.7), kind=kOutput, calls=%fused_computation.14 | convolution fusion | flops 1074003968 | bytes 5767168 | tf_op jit(solution)/shard_map/td,pde->pte/dot_general | solution.py:37
  75.9 0.0 copy-start.6
  75.9 0.0 copy-start.5
  75.9 0.9 pad_maximum_fusion
  76.9 0.0 all-gather.7.cloned.1.call-update
  76.9 0.0 reduce-scatter.2.cloned.1.call-start
  77.0 0.0 copy-done.6
  77.0 0.0 copy-done.5
  77.0 24.6 %all-gather.7.cloned.1.call-done = bf16[6,256,512]{2,1,0:T(8,128)(2,1)} async-done(((bf16[3,256,512]{2,1,0:T(8,128)(2,1)}), bf16[6,256,512]{2,1,0:T(8,128)(2,1)}) %all-gather.7.cloned.1.call-update) | async-done | bytes 1572880 | tf_op jit(solution)/shard_map/all_gather | solution.py:44
  101.6 2.6 %copy.17 = bf16[6,256,512]{1,2,0:T(8,128)(2,1)} copy(bf16[6,256,512]{2,1,0:T(8,128)(2,1)} %all-gather.7.cloned.1.call-done) | data formatting | bytes 3145728 | tf_op jit(solution)/shard_map/all_gather | solution.py:44
  104.2 1.7 convert_element_type.78
  105.9 0.3 fusion.34
  106.2 2.4 %fusion.11 = (f32[512]{0:T(512)S(1)}, f32[512]{0:T(512)S(1)}, f32[512]{0:T(512)S(1)}, f32[512]{0:T(512)}, f32[512]{0:T(512)S(1)}, /*index=5*/bf16[256,512]{0,1:T(8,128)(2,1)S(1)}, f32[256,512]{0,1:T(8,128)S(1)}) fusion(f32[256,512]{0,1:T(8,128)S(1)} %fusion.31, bf16[1,3,256,512]{2,3,1,0:T(8,128)(2,1)S(1)} %get-tuple-element.25, ...), kind=kLoop, calls=%fused_computation.35 | loop fusion | flops 4453888 | bytes 2379776 | tf_op jit(solution)/shard_map/reduce_sum | solution.py:70
  108.6 0.0 copy-start.2
  108.7 0.9 convolution_convert_fusion
  109.5 1.0 fusion.10
  110.6 0.4 copy-done.2
  111.0 0.8 fusion.2
  111.8 0.8 fusion
  112.5 0.3 copy.22
  112.8 0.3 copy.21
  113.2 0.2 maximum_bitcast_fusion
  113.4 1.8 copy.18
  115.2 0.0 reduce-scatter.2.cloned.1.call-update
  115.2 5.7 %convolution_bitcast_fusion = f32[2,2048,512]{1,2,0:T(8,128)} fusion(bf16[256,2048,1]{1,0,2:T(8,128)(2,1)} %reshape.57, bf16[1,256,512]{1,2,0:T(8,128)(2,1)S(1)} %bitcast.94, bf16[1,256,512]{1,2,0:T(8,128)(2,1)S(1)} %bitcast.93), kind=kOutput, calls=%fused_computation | convolution fusion | flops 1074003968 | bytes 9961472 | tf_op jit(solution)/shard_map/td,pte->pde/dot_general | solution.py:86
  120.9 55.5 %reduce-scatter.2.cloned.1.call-done = bf16[1,2,128,256]{3,2,1,0:T(8,128)(2,1)} async-done(((bf16[16,2,128,256]{3,2,1,0:T(8,128)(2,1)}), bf16[1,2,128,256]{3,2,1,0:T(8,128)(2,1)}) %reduce-scatter.2.cloned.1.call-update) | async-done | bytes 131088 | tf_op jit(solution)/shard_map/reduce_scatter | solution.py:82
  176.4 2.6 %collective-permute-start.1 = (bf16[2,128,256]{2,1,0:T(8,128)(2,1)}, bf16[2,128,256]{2,1,0:T(8,128)(2,1)S(1)}, u32[]{:S(2)}, u32[]{:S(2)}) collective-permute-start(bf16[2,128,256]{2,1,0:T(8,128)(2,1)} %bitcast.113), channel_id=1, source_target_pairs={{0,0},{16,1},{2,2},{18,3},{4,4},{20,5},{6,6},{22,7},{8,8},{24,9},{... | collective-permute-start | bytes 393224 | tf_op jit(solution)/shard_map/ppermute | solution.py:83
  179.0 4.3 %fusion.33 = f32[512,2048]{1,0:T(8,128)} fusion(bf16[256,2048]{1,0:T(8,128)(2,1)} %bitcast.97, bf16[1,3,256,512]{2,3,1,0:T(8,128)(2,1)S(1)} %get-tuple-element.25, f32[256,512]{0,1:T(8,128)} %copy-done.3), kind=kOutput, calls=%fused_computation.68 | convolution fusion | flops 538312704 | bytes 6029312 | tf_op jit(solution)/shard_map/dot_general | solution.py:89
  183.2 8.7 %copy.19 = f32[2,2048,512]{2,1,0:T(8,128)} copy(f32[2,2048,512]{1,2,0:T(8,128)} %convolution_bitcast_fusion) | data formatting | bytes 16777216
  191.9 0.6 pad_maximum_fusion.2
  192.5 0.0 collective-permute-done.1
  192.5 0.7 slice_bitcast_fusion.3
  (8 shorter events, 0.1 us)
Async XLA Ops:
  7.2 63.2 %copy-start = (bf16[512,2048]{1,0:T(8,128)(2,1)S(1)}, bf16[512,2048]{1,0:T(8,128)(2,1)}, u32[]{:S(2)}) copy-start(bf16[512,2048]{1,0:T(8,128)(2,1)} %param.10) | copy-start | bytes 6291460
  7.2 55.7 %all-gather.5.cloned.1.call-start = ((), (), s32[]{:S(2)}) async-start(), calls=%async_computation.2 | async-start | bytes 2228224 | tf_op jit(solution)/shard_map/all_gather | solution.py:32
  8.3 10.9 %collective-permute-start = (bf16[2,128,256]{2,1,0:T(8,128)(2,1)S(1)}, bf16[2,128,256]{2,1,0:T(8,128)(2,1)S(1)}, u32[]{:S(2)}, u32[]{:S(2)}) collective-permute-start(bf16[2,128,256]{2,1,0:T(8,128)(2,1)S(1)} %pad_maximum_fusion.1), channel_id=1, source_target_pairs={{0,0},{1,16},{2,2},{3,18},{4,4},{5,20},{6,6},{7,22},{8,8},{9,24},{... | collective-permute-start | bytes 393224 | tf_op jit(solution)/shard_map/ppermute | solution.py:31
  19.1 0.7 copy-start.4
  19.8 81.8 %all-gather.7.cloned.1.call-start = ((), (), s32[]{:S(2)}) async-start(), calls=%async_computation.3 | async-start | bytes 2359296 | tf_op jit(solution)/shard_map/all_gather | solution.py:44
  70.4 2.1 %copy-start.1 = (bf16[256,2048,1]{1,0,2:T(8,128)(2,1)S(1)}, bf16[256,2048,1]{1,0,2:T(8,128)(2,1)}, u32[]{:S(2)}) copy-start(bf16[256,2048,1]{1,0,2:T(8,128)(2,1)} %reshape.57) | copy-start | bytes 3145732
  75.9 1.1 copy-start.6
  75.9 1.1 copy-start.5
  76.9 99.5 %reduce-scatter.2.cloned.1.call-start = ((), (), s32[]{:S(2)}) async-start(), calls=%async_computation.1 | async-start | bytes 2228224 | tf_op jit(solution)/shard_map/reduce_scatter | solution.py:82
  108.6 0.9 copy-start.3
  108.6 2.4 %copy-start.2 = (bf16[2,2048,512]{2,1,0:T(8,128)(2,1)S(1)}, bf16[2,2048,512]{2,1,0:T(8,128)(2,1)}, u32[]{:S(2)}) copy-start(bf16[2,2048,512]{2,1,0:T(8,128)(2,1)} %param.7) | copy-start | bytes 12582916
  176.4 16.2 %collective-permute-start.1 = (bf16[2,128,256]{2,1,0:T(8,128)(2,1)}, bf16[2,128,256]{2,1,0:T(8,128)(2,1)S(1)}, u32[]{:S(2)}, u32[]{:S(2)}) collective-permute-start(bf16[2,128,256]{2,1,0:T(8,128)(2,1)} %bitcast.113), channel_id=1, source_target_pairs={{0,0},{16,1},{2,2},{18,3},{4,4},{20,5},{6,6},{22,7},{8,8},{24,9},{... | collective-permute-start | bytes 393224 | tf_op jit(solution)/shard_map/ppermute | solution.py:83
Sparse Core Ops, SparseCore 0:
  19.9 42.8 all-gather.4
  77.0 24.5 all-gather.6
  115.3 60.9 reduce-scatter.1

commit v2 on v1

v2 whole, which is shorter than its diff:
```python
import functools

import jax
import jax.numpy as jnp
from jax import lax
from jax.experimental import pallas as pl
from jax.experimental.pallas import tpu as pltpu
from jax.sharding import PartitionSpec as P

F32, BF16 = jnp.float32, jnp.bfloat16
MESH = pl.DeviceIdType.MESH
NT = (((1,), (1,)), ((), ()))
TN = (((0,), (0,)), ((), ()))


def silu_parts(value):
    sig = jax.nn.sigmoid(value)
    return (value * sig, sig * (1.0 + value * (1.0 - sig)))


def split_dp(n):
    pairs = n // 2
    ys = 2 ** ((pairs.bit_length() - 1) // 2)
    return pairs // ys, ys


def body(
    n, m, tok, gout, win_hbm, cw_ref, cb_ref, wout_hbm,
    out_ref, gtok_ref, x_ref, g_ref, hid_ref, gi_ref, gg_ref, tap_ref, bias_ref,
    win, wout, pack, gat, slot, part, rcore, ry, rz, fin, res, pad, pad2,
    w_sem, sw_send, sw_recv, gz_send, gy_send, gc_send, g_recv, ex_send, ex_recv,
    rc_send, rc_recv, ry_send, ry_recv, rz_send, rz_recv,
):
    zs, ys = split_dp(n)
    per = n // m
    rows, cols = tok.shape
    total = rows * m
    taps, chans = cw_ref.shape
    chunks, width = slot.shape[1], slot.shape[4]
    dp, seq = lax.axis_index("dp"), lax.axis_index("seq")
    z, y, c = dp // (2 * ys), (dp // 2) % ys, dp % 2
    other = 1 - c

    def at(zz, yy, cc):
        return (zz * ys + yy) * 2 + cc

    mate = {"dp": seq * per + dp % per, "seq": dp // per}
    swaps = dp // per != seq

    def send(src, dst, ssem, rsem, where):
        return pltpu.make_async_remote_copy(
            src_ref=src, dst_ref=dst, send_sem=ssem, recv_sem=rsem,
            device_id=where, device_id_type=MESH,
        )

    loads = [
        pltpu.make_async_copy(win_hbm, win, w_sem.at[0]),
        pltpu.make_async_copy(wout_hbm, wout, w_sem.at[1]),
    ]
    for load in loads:
        load.start()

    barrier = pltpu.get_barrier_semaphore()
    near = [{"dp": at(z, y, other)}]
    near += [{"dp": at(z, (y + d) % ys, c)} for d in range(1, ys)]
    near += [{"dp": at((z + d) % zs, y, c)} for d in range(1, zs)]
    near += [{"seq": (seq + d) % m} for d in range(1, m)]
    for where in near:
        pl.semaphore_signal(barrier, inc=1, device_id=where, device_id_type=MESH)

    @pl.when(swaps)
    def _():
        pl.semaphore_signal(barrier, inc=1, device_id=mate, device_id_type=MESH)

    pl.semaphore_wait(barrier, len(near) + swaps.astype(jnp.int32))

    @pl.when(swaps)
    def _():
        pack[0] = tok[...]
        pack[1] = gout[...]
        copy = send(pack, gat.at[mate["dp"]], sw_send.at[0], sw_recv.at[0], mate)
        copy.start()
        copy.wait_send()
        send(pack, gat.at[dp], sw_send.at[0], sw_recv.at[0], mate).wait_recv()

    @pl.when(jnp.logical_not(swaps))
    def _():
        gat[dp, 0] = tok[...]
        gat[dp, 1] = gout[...]

    def arrived(q):
        send(gat.at[q], gat.at[q], gc_send.at[0], g_recv.at[q], mate).wait_recv()

    sent = []

    def forward(q, ssem, where):
        copy = send(gat.at[q], gat.at[q], ssem, g_recv.at[q], where)
        copy.start()
        sent.append(copy)

    for d in range(1, zs):
        forward(dp, gz_send.at[d - 1], {"dp": at((z + d) % zs, y, c)})
    for d in range(zs):
        q = at((z + d) % zs, y, c)
        if d:
            arrived(q)
        for e in range(1, ys):
            forward(q, gy_send.at[d * (ys - 1) + e - 1], {"dp": at(z, (y + e) % ys, c)})
        forward(q, gc_send.at[d * ys], {"dp": at(z, y, other)})
    for d in range(zs):
        for e in range(1, ys):
            q = at((z + d) % zs, (y + e) % ys, c)
            arrived(q)
            forward(q, gc_send.at[d * ys + e], {"dp": at(z, y, other)})
    for d in range(zs):
        for e in range(ys):
            arrived(at((z + d) % zs, (y + e) % ys, other))
    for q in range(n):
        t, j = q // per, q % per
        x_ref[t * rows : (t + 1) * rows, j * cols : (j + 1) * cols] = gat[q, 0]
        g_ref[t * rows : (t + 1) * rows, j * cols : (j + 1) * cols] = gat[q, 1]
    for load in loads:
        load.wait()

    for k in range(chunks):
        span = slice(k * width, (k + 1) * width)
        for p in range(2):
            slot[seq, k, p] = jnp.dot(
                x_ref[...], win[p, :, span], preferred_element_type=F32
            ).astype(BF16)
        slot[seq, k, 2] = lax.dot_general(
            g_ref[...], wout[span, :], NT, preferred_element_type=F32
        ).astype(BF16)
        for d in range(1, m):
            copy = send(
                slot.at[seq, k], slot.at[seq, k], ex_send.at[k * (m - 1) + d - 1],
                ex_recv.at[k * m + seq], {"seq": (seq + d) % m},
            )
            copy.start()
            sent.append(copy)

    pad[0:8] = jnp.zeros((8, pad.shape[1]), F32)
    pad2[total : total + 8] = jnp.zeros((8, pad.shape[1]), F32)
    lanes = pad.shape[1]
    taps_f = cw_ref[...].astype(F32)
    shift_f = cb_ref[...].astype(F32)
    for k in range(chunks):
        for d in range(1, m):
            peer = (seq + d) % m
            send(
                slot.at[peer, k], slot.at[peer, k], ex_send.at[0],
                ex_recv.at[k * m + peer], mate,
            ).wait_recv()
        for col in range(0, width, lanes):
            local = slice(col, col + lanes)
            span = slice(k * width + col, k * width + col + lanes)

            def summed(p):
                value = slot[0, k, p, :, local].astype(F32)
                for i in range(1, m):
                    value = value + slot[i, k, p, :, local].astype(F32)
                return value

            pad[8 : 8 + total] = summed(0).astype(BF16).astype(F32)
            gate, gate_slope = silu_parts(summed(1).astype(BF16).astype(F32))
            conv = jnp.broadcast_to(shift_f[:, span], (total, lanes))
            for lag in range(taps):
                first = 9 - taps + lag
                conv = conv + taps_f[lag : lag + 1, span] * pad[first : first + total]
            act, act_slope = silu_parts(conv)
            back = summed(2)
            hid_ref[:, span] = (act * gate).astype(BF16)
            gg_ref[:, span] = (back * act * gate_slope).astype(BF16)
            grad_conv = (back * gate * act_slope).astype(BF16).astype(F32)
            pad2[0:total] = grad_conv
            grad_inner = jnp.zeros((total, lanes), F32)
            for lag in range(taps):
                first = taps - 1 - lag
                grad_inner = grad_inner + taps_f[lag : lag + 1, span] * pad2[first : first + total]
            gi_ref[:, span] = grad_inner.astype(BF16)
            for lag in range(taps):
                first = 9 - taps + lag
                tap_ref[lag : lag + 1, span] = jnp.sum(
                    grad_conv * pad[first : first + total], axis=0, keepdims=True
                )
            bias_ref[:, span] = jnp.sum(grad_conv, axis=0, keepdims=True)

    for j in range(per):
        span = slice(j * cols, (j + 1) * cols)
        first = jnp.dot(hid_ref[...], wout[:, span], preferred_element_type=F32)
        second = lax.dot_general(gi_ref[...], win[0, span, :], NT, preferred_element_type=F32)
        second = second + lax.dot_general(
            gg_ref[...], win[1, span, :], NT, preferred_element_type=F32
        )
        for t in range(m):
            part[t * per + j, 0] = first[t * rows : (t + 1) * rows].astype(BF16)
            part[t * per + j, 1] = second[t * rows : (t + 1) * rows].astype(BF16)

    order = [(d, e) for e in range(ys - 1, -1, -1) for d in range(zs - 1, -1, -1)]

    def core_copy(d, e, which):
        zz, yy = (z + d) % zs, (y + e) % ys
        i = zz * ys + yy
        return send(part.at[at(zz, yy, which)], rcore.at[i], rc_send.at[i], rc_recv.at[i],
                    {"dp": at(z, y, other)})

    for d, e in order:
        copy = core_copy(d, e, other)
        copy.start()
        sent.append(copy)
    for e in range(ys - 1, 0, -1):
        for d in range(zs - 1, -1, -1):
            zz, yy = (z + d) % zs, (y + e) % ys
            core_copy(d, e, other).wait_recv()
            q = at(zz, yy, c)
            part[q] = (part[q].astype(F32) + rcore[zz * ys + yy].astype(F32)).astype(BF16)
            i = (e - 1) * zs + zz
            copy = send(part.at[q], ry.at[i], ry_send.at[i], ry_recv.at[i], {"dp": at(z, yy, c)})
            copy.start()
            sent.append(copy)
    for d in range(zs - 1, -1, -1):
        zz = (z + d) % zs
        core_copy(d, 0, other).wait_recv()
        q = at(zz, y, c)
        value = part[q].astype(F32) + rcore[zz * ys + y].astype(F32)
        for e in range(1, ys):
            i = (e - 1) * zs + zz
            send(part.at[q], ry.at[i], ry_send.at[i], ry_recv.at[i], mate).wait_recv()
            value = value + ry[i].astype(F32)
        if d:
            part[q] = value.astype(BF16)
            copy = send(part.at[q], rz.at[d - 1], rz_send.at[d - 1], rz_recv.at[d - 1],
                        {"dp": at(zz, y, c)})
            copy.start()
            sent.append(copy)
        else:
            for i in range(zs - 1):
                send(part.at[q], rz.at[i], rz_send.at[i], rz_recv.at[i], mate).wait_recv()
                value = value + rz[i].astype(F32)
            fin[...] = value.astype(BF16)

    @pl.when(swaps)
    def _():
        copy = send(fin, res, sw_send.at[1], sw_recv.at[1], mate)
        copy.start()
        copy.wait()
        out_ref[...] = res[0]
        gtok_ref[...] = res[1]

    @pl.when(jnp.logical_not(swaps))
    def _():
        out_ref[...] = fin[0]
        gtok_ref[...] = fin[1]

    for copy in sent:
        copy.wait_send()


def weight_grads(x_ref, g_ref, hid_ref, gi_ref, gg_ref, din_ref, dout_ref):
    x = x_ref[...]
    din_ref[0] = lax.dot_general(x, gi_ref[...], TN, preferred_element_type=F32)
    din_ref[1] = lax.dot_general(x, gg_ref[...], TN, preferred_element_type=F32)
    dout_ref[...] = lax.dot_general(hid_ref[...], g_ref[...], TN, preferred_element_type=F32)


def on_device(tokens, in_weight, conv_weight, conv_bias, out_weight, grad_out):
    n, m = lax.axis_size("dp"), lax.axis_size("seq")
    zs, ys = split_dp(n)
    rows, cols = tokens.shape
    total = rows * m
    depth = in_weight.shape[1]
    taps, chans = conv_weight.shape
    width = min(chans, 256)
    chunks = chans // width
    lanes = min(width, 128)
    vmem = pl.BlockSpec(memory_space=pltpu.VMEM)
    hbm = pl.BlockSpec(memory_space=pl.ANY)
    dma = lambda count: pltpu.SemaphoreType.DMA((max(count, 1),))
    pair = (2, rows, cols)
    shape = jax.ShapeDtypeStruct
    flops = 2 * total * depth * chans * 6
    out, gtok, x, g, hid, gi, gg, tap, bias = pl.pallas_call(
        functools.partial(body, n, m),
        out_shape=(
            shape((rows, cols), BF16), shape((rows, cols), BF16),
            shape((total, depth), BF16), shape((total, depth), BF16),
            shape((total, chans), BF16), shape((total, chans), BF16),
            shape((total, chans), BF16),
            shape((taps, chans), F32), shape((1, chans), F32),
        ),
        in_specs=[vmem, vmem, hbm, vmem, vmem, hbm],
        out_specs=(vmem,) * 9,
        scratch_shapes=[
            pltpu.VMEM(in_weight.shape, BF16),
            pltpu.VMEM(out_weight.shape, BF16),
            pltpu.VMEM(pair, BF16),
            pltpu.VMEM((n,) + pair, BF16),
            pltpu.VMEM((m, chunks, 3, total, width), BF16),
            pltpu.VMEM((n,) + pair, BF16),
            pltpu.VMEM((zs * ys,) + pair, BF16),
            pltpu.VMEM((max(zs * (ys - 1), 1),) + pair, BF16),
            pltpu.VMEM((max(zs - 1, 1),) + pair, BF16),
            pltpu.VMEM(pair, BF16),
            pltpu.VMEM(pair, BF16),
            pltpu.VMEM((total + 8, lanes), F32),
            pltpu.VMEM((total + 8, lanes), F32),
            dma(2), dma(2), dma(2),
            dma(zs - 1), dma(zs * (ys - 1)), dma(zs * ys), dma(n),
            dma(chunks * (m - 1)), dma(chunks * m),
            dma(zs * ys), dma(zs * ys),
            dma(zs * (ys - 1)), dma(zs * (ys - 1)),
            dma(zs - 1), dma(zs - 1),
        ],
        compiler_params=pltpu.CompilerParams(
            collective_id=0, has_side_effects=True, vmem_limit_bytes=56 * 2**20
        ),
        cost_estimate=pl.CostEstimate(
            flops=flops, bytes_accessed=12 * 2**20, transcendentals=2 * total * chans
        ),
        name="mixer",
    )(tokens, grad_out, in_weight, conv_weight, conv_bias.reshape(1, chans), out_weight)

    tile = min(depth, 256)
    whole = pl.BlockSpec((total, chans), lambda i: (0, 0))
    strip = pl.BlockSpec((total, tile), lambda i: (0, i))
    din, dout = pl.pallas_call(
        weight_grads,
        grid=(depth // tile,),
        out_shape=(shape(in_weight.shape, F32), shape(out_weight.shape, F32)),
        in_specs=[strip, strip, whole, whole, whole],
        out_specs=(
            pl.BlockSpec((2, tile, chans), lambda i: (0, i, 0)),
            pl.BlockSpec((chans, tile), lambda i: (0, i)),
        ),
        compiler_params=pltpu.CompilerParams(vmem_limit_bytes=32 * 2**20),
        name="weight_grads",
    )(x, g, hid, gi, gg)
    return (out, gtok, din, dout, tap, bias.reshape(chans))


def solution(mesh):
    return jax.shard_map(
        on_device,
        mesh=mesh,
        in_specs=(
            P("seq", "dp"),
            P(None, "seq", "dp"),
            P(None, "dp"),
            P("dp"),
            P("dp", "seq"),
            P("seq", "dp"),
        ),
        out_specs=(
            P("seq", "dp"),
            P("seq", "dp"),
            P(None, "seq", "dp"),
            P("dp", "seq"),
            P(None, "dp"),
            P("dp"),
        ),
        check_vma=False,
    )
```

time: 203 us -> 98 us (0.48); the launches traced: 200 us -> 97.4 us
  waiting for transfers between devices: 130 us -> 0 us
  Pallas kernels: 0 us -> 84.7 us
  matrix products: 17.9 us -> 0 us
  between operations: 13.9 us -> 0.65 us
  local copies, waits for them, and re-layouts: 23 us -> 12 us
  other arithmetic: 8.23 us -> 0 us
  starting transfers between devices: 6.91 us -> 0 us
    pallas_call x0 -> x2, Pallas kernels: none -> 84.7 us  [the longest x1 78 us: on_device(): pl.pallas_call(functools.partial(body, n, m), out_shape=(shape((rows, col...]
    all_gather x2 -> x0, waiting for transfers between devices: 67.6 us -> none  [the longest x1 43 us: on_device(): gathered = lax.all_gather(moved, 'dp')]
    reduce_scatter x1 -> x0, waiting for transfers between devices: 55.5 us -> none  [on_device(): summed = lax.psum_scatter(sent, 'dp', scatter_dimension=0, tiled=False)]
    dot_general x7 -> x0, matrix products: 17.9 us -> none  [the longest x1 5.71 us: on_device(): jnp.einsum('td,pte->pde', whole, branch, preferred_element_type=jnp.float32)]
    ppermute x2 -> x0, starting transfers between devices: 6.79 us -> none  [the longest x1 4.19 us: on_device(): moved = lax.ppermute(both, ('dp', 'seq'), there)]
    ppermute x2 -> x0, waiting for transfers between devices: 6.69 us -> none  [the longest x1 6.69 us: on_device(): moved = lax.ppermute(both, ('dp', 'seq'), there)]
    squeeze x2 -> x0, local copies, waits for them, and re-layouts: 3.03 us -> none  [the longest x1 2.37 us: on_device(): whole, upstream = (arranged[0], arranged[1])]
    convert_element_type x5 -> x0, other arithmetic: 2.78 us -> none  [the longest x1 1.69 us: on_device(): parts = lax.all_gather(parts, 'seq').astype(jnp.float32)]
  transfers between devices with their start and end apart: 5 -> 0, of which waited for: 4 -> 0; matrix products, arithmetic and copies ran while one was open for 10% -> 0% of each run, Pallas kernels for 0% -> 0%
where the time goes in v2:
time: 98 us; the launch traced here: 97.4 us
  Pallas kernels  84.7 us (86%)
  local copies, waits for them, and re-layouts  12 us (12%)
    pallas_call x1, Pallas kernels, on_device(): pl.pallas_call(functools.partial(body, n, m), out_shape=(shape((rows, col...  78 us
    unnamed x14, local copies, waits for them, and re-layouts  10.8 us
    pallas_call x1, Pallas kernels, on_device(): pl.pallas_call(weight_grads, grid=(depth // tile,), out_shape=(shape(in_w...  6.75 us

profile of v2, /device:TPU:3, one launch (start us, length us, event | category | flops | bytes accessed | tf_op | source)
XLA Modules:
  0.0 97.4 jit_solution(13630746367628880069)
XLA Ops:
  0.6 1.3 %reshape.18.cb_ref = bf16[1,512]{1,0:T(2,128)(2,1)} reshape(bf16[512]{0:T(512)(128)(2,1)} %param.9) | data formatting | bytes 2048 | tf_op jit(solution)/shard_map/reshape | solution.py:321
  1.9 78.0 %mixer.1 = (bf16[128,256]{1,0:T(8,128)(2,1)}, bf16[128,256]{1,0:T(8,128)(2,1)}, bf16[256,2048]{1,0:T(8,128)(2,1)}, bf16[256,2048]{1,0:T(8,128)(2,1)}, bf16[256,5...) custom-call(bf16[128,256]{1,0:T(8,128)(2,1)} %tok.1, ...), custom_call_target="tpu_custom_call" | custom-call | flops 3221225472 | bytes 12582912 | tf_op jit(solution)/shard_map/mixer/pallas_call | solution.py:282
  79.9 0.0 copy-start
  79.9 1.2 %copy-done = bf16[256,2048]{1,0:T(8,128)(2,1)S(1)} copy-done((bf16[256,2048]{1,0:T(8,128)(2,1)S(1)}, bf16[256,2048]{1,0:T(8,128)(2,1)}, u32[]{:S(2)}) %copy-start) | copy-done | bytes 1048600
  81.1 0.0 copy-start.1
  81.1 1.2 %copy-done.1 = bf16[256,2048]{1,0:T(8,128)(2,1)S(1)} copy-done((bf16[256,2048]{1,0:T(8,128)(2,1)S(1)}, bf16[256,2048]{1,0:T(8,128)(2,1)}, u32[]{:S(2)}) %copy-start.1) | copy-done | bytes 1048600
  82.3 0.0 copy-start.2
  82.3 0.9 copy-done.2
  83.3 0.0 copy-start.3
  83.3 0.9 copy-done.3
  84.2 0.0 copy-start.4
  84.2 0.9 copy-done.4
  85.2 6.8 %weight_grads.1 = (f32[2,2048,512]{2,1,0:T(8,128)}, f32[512,2048]{1,0:T(8,128)}) custom-call(bf16[256,2048]{1,0:T(8,128)(2,1)S(1)} %copy-done, bf16[256,2048]{1,0:T(8,128)(2,1)S(1)} %copy-done.1, bf16[256,512]{1,0:T(8,128)(2,1)S(1)} %copy-done.2, bf16[256,512]{1,0:T(8,128)(2,1)S(1)} %copy-done.3, bf16[256,512]{1,0:T(8,128)(2,1)S(1)} %copy-done.4), custom_call_target="tpu_custom_call" | custom-call | tf_op jit(solution)/shard_map/weight_grads/pallas_call | solution.py:326
  91.9 1.5 %copy.16 = bf16[128,256]{1,0:T(8,128)(2,1)} copy(bf16[128,256]{1,0:T(8,128)(2,1)} %get-tuple-element.34) | data formatting | bytes 131072
  93.4 1.5 %copy.17 = bf16[128,256]{1,0:T(8,128)(2,1)} copy(bf16[128,256]{1,0:T(8,128)(2,1)} %get-tuple-element.35) | data formatting | bytes 131072
  94.8 1.3 %copy.18 = f32[4,512]{1,0:T(4,128)} copy(f32[4,512]{1,0:T(4,128)} %get-tuple-element.38) | data formatting | bytes 16384
  96.1 1.2 %copy.19 = f32[512]{0:T(512)} copy(f32[512]{0:T(512)} %bitcast.1) | data formatting | bytes 4096
Async XLA Ops:
  79.9 1.2 %copy-start = (bf16[256,2048]{1,0:T(8,128)(2,1)S(1)}, bf16[256,2048]{1,0:T(8,128)(2,1)}, u32[]{:S(2)}) copy-start(bf16[256,2048]{1,0:T(8,128)(2,1)} %get-tuple-element.19.x_ref) | copy-start | bytes 3145732
  81.1 1.2 %copy-start.1 = (bf16[256,2048]{1,0:T(8,128)(2,1)S(1)}, bf16[256,2048]{1,0:T(8,128)(2,1)}, u32[]{:S(2)}) copy-start(bf16[256,2048]{1,0:T(8,128)(2,1)} %get-tuple-element.20.g_ref) | copy-start | bytes 3145732
  82.3 0.9 copy-start.2
  83.3 0.9 copy-start.3
  84.2 0.9 copy-start.4

commit v3 on v2

v3 whole, which is shorter than its diff:
```python
import functools

import jax
import jax.numpy as jnp
from jax import lax
from jax.experimental import pallas as pl
from jax.experimental.pallas import tpu as pltpu
from jax.sharding import PartitionSpec as P

F32, BF16 = jnp.float32, jnp.bfloat16
MESH = pl.DeviceIdType.MESH
NT = (((1,), (1,)), ((), ()))
TN = (((0,), (0,)), ((), ()))


def silu_parts(value):
    sig = jax.nn.sigmoid(value)
    return (value * sig, sig * (1.0 + value * (1.0 - sig)))


def split_dp(n):
    pairs = n // 2
    ys = 2 ** ((pairs.bit_length() - 1) // 2)
    return pairs // ys, ys


def body(
    n, m, tok, gout, win_hbm, cw_ref, cb_ref, wout_hbm,
    out_ref, gtok_ref, x_ref, g_ref, hid_ref, gi_ref, gg_ref, tap_ref, bias_ref,
    win, wout, gat, slot, bslot, part, rcore, ry, rz, fin, res, pad, pad2, sa, sb,
    w_sem, sw_send, sw_recv, gz_send, gy_send, gc_send, g_recv, ex_send, ex_recv,
    bx_send, bx_recv, rc_send, rc_recv, ry_send, ry_recv, rz_send, rz_recv,
):
    zs, ys = split_dp(n)
    per = n // m
    rows, cols = tok.shape
    total = rows * m
    taps, chans = cw_ref.shape
    chunks, width = slot.shape[1], slot.shape[4]
    lanes = pad2.shape[1]
    dp, seq = lax.axis_index("dp"), lax.axis_index("seq")
    z, y, c = dp // (2 * ys), (dp // 2) % ys, dp % 2
    other = 1 - c

    def at(zz, yy, cc):
        return (zz * ys + yy) * 2 + cc

    mate = {"dp": seq * per + dp % per, "seq": dp // per}
    swaps = dp // per != seq

    def send(src, dst, ssem, rsem, where):
        return pltpu.make_async_remote_copy(
            src_ref=src, dst_ref=dst, send_sem=ssem, recv_sem=rsem,
            device_id=where, device_id_type=MESH,
        )

    loads = [
        pltpu.make_async_copy(win_hbm, win, w_sem.at[0]),
        pltpu.make_async_copy(wout_hbm, wout, w_sem.at[1]),
    ]
    for load in loads:
        load.start()

    barrier = pltpu.get_barrier_semaphore()
    near = [{"dp": at(z, y, other)}]
    near += [{"dp": at(z, (y + d) % ys, c)} for d in range(1, ys)]
    near += [{"dp": at((z + d) % zs, y, c)} for d in range(1, zs)]
    near += [{"seq": (seq + d) % m} for d in range(1, m)]
    for where in near:
        pl.semaphore_signal(barrier, inc=1, device_id=where, device_id_type=MESH)

    @pl.when(swaps)
    def _():
        pl.semaphore_signal(barrier, inc=1, device_id=mate, device_id_type=MESH)

    pl.semaphore_wait(barrier, len(near) + swaps.astype(jnp.int32))

    sent = []

    def go(*args):
        copy = send(*args)
        copy.start()
        sent.append(copy)

    def gathered(p, q, ssem, where):
        go(gat.at[p, q], gat.at[p, q], ssem, g_recv.at[p, q], where)

    def arrived(p, q):
        here = gat.at[p, q]
        send(here, here, gc_send.at[p, 0], g_recv.at[p, q], mate).wait_recv()

    sources = (tok, gout)

    def swap_in(p):
        return send(sources[p], gat.at[p, mate["dp"]], sw_send.at[p], sw_recv.at[p], mate)

    @pl.when(swaps)
    def _():
        for p in range(2):
            swap_in(p).start()
        for p in range(2):
            swap_in(p).wait_send()

    def own_block(p):
        @pl.when(swaps)
        def _():
            send(gat.at[p, dp], gat.at[p, dp], sw_send.at[p], sw_recv.at[p], mate).wait_recv()

        @pl.when(jnp.logical_not(swaps))
        def _():
            gat[p, dp] = sources[p][...]

        for d in range(1, zs):
            gathered(p, dp, gz_send.at[p, d - 1], {"dp": at((z + d) % zs, y, c)})

    def along_z(p):
        for d in range(zs):
            q = at((z + d) % zs, y, c)
            if d:
                arrived(p, q)
            for e in range(1, ys):
                i = d * (ys - 1) + e - 1
                gathered(p, q, gy_send.at[p, i], {"dp": at(z, (y + e) % ys, c)})
            gathered(p, q, gc_send.at[p, d * ys], {"dp": at(z, y, other)})

    def along_y(p, dest):
        for d in range(zs):
            for e in range(1, ys):
                q = at((z + d) % zs, (y + e) % ys, c)
                arrived(p, q)
                gathered(p, q, gc_send.at[p, d * ys + e], {"dp": at(z, y, other)})
        for d in range(zs):
            for e in range(ys):
                arrived(p, at((z + d) % zs, (y + e) % ys, other))
        for q in range(n):
            t, j = q // per, q % per
            dest[t * rows : (t + 1) * rows, j * cols : (j + 1) * cols] = gat[p, q]

    own_block(0)
    along_z(0)
    own_block(1)
    along_y(0, x_ref)
    for load in loads:
        load.wait()

    for k in range(chunks):
        span = slice(k * width, (k + 1) * width)
        for p in range(2):
            slot[seq, k, p] = jnp.dot(
                x_ref[...], win[p, :, span], preferred_element_type=F32
            ).astype(BF16)
        for d in range(1, m):
            here = slot.at[seq, k]
            go(here, here, ex_send.at[k * (m - 1) + d - 1], ex_recv.at[k * m + seq],
               {"seq": (seq + d) % m})
    along_z(1)
    along_y(1, g_ref)
    for k in range(chunks):
        span = slice(k * width, (k + 1) * width)
        bslot[seq, :, span] = lax.dot_general(
            g_ref[...], wout[span, :], NT, preferred_element_type=F32
        ).astype(BF16)
    for d in range(1, m):
        here = bslot.at[seq]
        go(here, here, bx_send.at[d - 1], bx_recv.at[seq], {"seq": (seq + d) % m})

    def over_seq(read):
        value = read(0).astype(F32)
        for i in range(1, m):
            value = value + read(i).astype(F32)
        return value

    pad[0:8] = jnp.zeros((8, chans), F32)
    pad2[total : total + 8] = jnp.zeros((8, lanes), F32)
    taps_f = cw_ref[...].astype(F32)
    shift_f = cb_ref[...].astype(F32)
    for k in range(chunks):
        for d in range(1, m):
            peer = (seq + d) % m
            here = slot.at[peer, k]
            send(here, here, ex_send.at[0], ex_recv.at[k * m + peer], mate).wait_recv()
        for col in range(0, width, lanes):
            local = slice(col, col + lanes)
            span = slice(k * width + col, k * width + col + lanes)
            inner = over_seq(lambda i: slot[i, k, 0, :, local])
            pad[8 : 8 + total, span] = inner.astype(BF16).astype(F32)
            gate_in = over_seq(lambda i: slot[i, k, 1, :, local])
            gate, gate_slope = silu_parts(gate_in.astype(BF16).astype(F32))
            conv = jnp.broadcast_to(shift_f[:, span], (total, lanes))
            for lag in range(taps):
                first = 9 - taps + lag
                conv = conv + taps_f[lag : lag + 1, span] * pad[first : first + total, span]
            act, act_slope = silu_parts(conv)
            hid_ref[:, span] = (act * gate).astype(BF16)
            sa[:, span] = gate * act_slope
            sb[:, span] = act * gate_slope

    def core_copy(p, d, e, which):
        zz, yy = (z + d) % zs, (y + e) % ys
        i = zz * ys + yy
        return send(part.at[p, at(zz, yy, which)], rcore.at[p, i], rc_send.at[p, i],
                    rc_recv.at[p, i], {"dp": at(z, y, other)})

    def to_core(p):
        for e in range(ys - 1, -1, -1):
            for d in range(zs - 1, -1, -1):
                copy = core_copy(p, d, e, other)
                copy.start()
                sent.append(copy)

    def to_y(p):
        for e in range(ys - 1, 0, -1):
            for d in range(zs - 1, -1, -1):
                zz, yy = (z + d) % zs, (y + e) % ys
                core_copy(p, d, e, other).wait_recv()
                q = at(zz, yy, c)
                value = part[p, q].astype(F32) + rcore[p, zz * ys + yy].astype(F32)
                part[p, q] = value.astype(BF16)
                i = (e - 1) * zs + zz
                go(part.at[p, q], ry.at[p, i], ry_send.at[p, i], ry_recv.at[p, i],
                   {"dp": at(z, yy, c)})

    def to_z(p):
        for d in range(zs - 1, -1, -1):
            zz = (z + d) % zs
            core_copy(p, d, 0, other).wait_recv()
            q = at(zz, y, c)
            value = part[p, q].astype(F32) + rcore[p, zz * ys + y].astype(F32)
            for e in range(1, ys):
                i = (e - 1) * zs + zz
                send(part.at[p, q], ry.at[p, i], ry_send.at[p, i], ry_recv.at[p, i],
                     mate).wait_recv()
                value = value + ry[p, i].astype(F32)
            if d:
                part[p, q] = value.astype(BF16)
                go(part.at[p, q], rz.at[p, d - 1], rz_send.at[p, d - 1], rz_recv.at[p, d - 1],
                   {"dp": at(zz, y, c)})
            else:
                part[p, q] = value.astype(BF16)

    def swap_out(p):
        return send(fin.at[p], res.at[p], sw_send.at[2 + p], sw_recv.at[2 + p], mate)

    def finish(p):
        value = part[p, dp].astype(F32)
        for i in range(zs - 1):
            send(part.at[p, dp], rz.at[p, i], rz_send.at[p, i], rz_recv.at[p, i],
                 mate).wait_recv()
            value = value + rz[p, i].astype(F32)
        fin[p] = value.astype(BF16)

        @pl.when(swaps)
        def _():
            swap_out(p).start()

    for j in range(per):
        span = slice(j * cols, (j + 1) * cols)
        value = jnp.dot(hid_ref[...], wout[:, span], preferred_element_type=F32)
        for t in range(m):
            part[0, t * per + j] = value[t * rows : (t + 1) * rows].astype(BF16)
    to_core(0)
    to_y(0)

    for d in range(1, m):
        here = bslot.at[(seq + d) % m]
        send(here, here, bx_send.at[0], bx_recv.at[(seq + d) % m], mate).wait_recv()
    for col in range(0, chans, lanes):
        span = slice(col, col + lanes)
        back = over_seq(lambda i: bslot[i, :, span])
        gg_ref[:, span] = (back * sb[:, span]).astype(BF16)
        grad_conv = (back * sa[:, span]).astype(BF16).astype(F32)
        pad2[0:total] = grad_conv
        grad_inner = jnp.zeros((total, lanes), F32)
        for lag in range(taps):
            first = taps - 1 - lag
            grad_inner = grad_inner + taps_f[lag : lag + 1, span] * pad2[first : first + total]
        gi_ref[:, span] = grad_inner.astype(BF16)
        for lag in range(taps):
            first = 9 - taps + lag
            tap_ref[lag : lag + 1, span] = jnp.sum(
                grad_conv * pad[first : first + total, span], axis=0, keepdims=True
            )
        bias_ref[:, span] = jnp.sum(grad_conv, axis=0, keepdims=True)
    for j in range(per):
        span = slice(j * cols, (j + 1) * cols)
        value = lax.dot_general(gi_ref[...], win[0, span, :], NT, preferred_element_type=F32)
        value = value + lax.dot_general(
            gg_ref[...], win[1, span, :], NT, preferred_element_type=F32
        )
        for t in range(m):
            part[1, t * per + j] = value[t * rows : (t + 1) * rows].astype(BF16)
    to_core(1)
    to_z(0)
    to_y(1)
    finish(0)
    to_z(1)
    finish(1)

    @pl.when(swaps)
    def _():
        for p in range(2):
            swap_out(p).wait()
        out_ref[...] = res[0]
        gtok_ref[...] = res[1]

    @pl.when(jnp.logical_not(swaps))
    def _():
        out_ref[...] = fin[0]
        gtok_ref[...] = fin[1]

    for copy in sent:
        copy.wait_send()


def weight_grads(
    x_ref, g_ref, hid_ref, gi_ref, gg_ref, out_in, tok_in, tap_in, bias_in,
    din_ref, dout_ref, out_ref, tok_ref, tap_ref, bias_ref,
):
    x = x_ref[...]
    din_ref[0] = lax.dot_general(x, gi_ref[...], TN, preferred_element_type=F32)
    din_ref[1] = lax.dot_general(x, gg_ref[...], TN, preferred_element_type=F32)
    dout_ref[...] = lax.dot_general(hid_ref[...], g_ref[...], TN, preferred_element_type=F32)
    out_ref[...] = out_in[...]
    tok_ref[...] = tok_in[...]
    tap_ref[...] = tap_in[...]
    bias_ref[...] = bias_in[0]


def on_device(tokens, in_weight, conv_weight, conv_bias, out_weight, grad_out):
    n, m = lax.axis_size("dp"), lax.axis_size("seq")
    zs, ys = split_dp(n)
    rows, cols = tokens.shape
    total = rows * m
    depth = in_weight.shape[1]
    taps, chans = conv_weight.shape
    width = min(chans, 256)
    chunks = chans // width
    lanes = min(width, 128)
    vmem = pl.BlockSpec(memory_space=pltpu.VMEM)
    hbm = pl.BlockSpec(memory_space=pl.ANY)
    dma = lambda *counts: pltpu.SemaphoreType.DMA(tuple(max(i, 1) for i in counts))
    block = (rows, cols)
    shape = jax.ShapeDtypeStruct
    flops = 2 * total * depth * chans * 6
    out, gtok, x, g, hid, gi, gg, tap, bias = pl.pallas_call(
        functools.partial(body, n, m),
        out_shape=(
            shape((rows, cols), BF16), shape((rows, cols), BF16),
            shape((total, depth), BF16), shape((total, depth), BF16),
            shape((total, chans), BF16), shape((total, chans), BF16),
            shape((total, chans), BF16),
            shape((taps, chans), F32), shape((1, chans), F32),
        ),
        in_specs=[vmem, vmem, hbm, vmem, vmem, hbm],
        out_specs=(vmem,) * 9,
        scratch_shapes=[
            pltpu.VMEM(in_weight.shape, BF16),
            pltpu.VMEM(out_weight.shape, BF16),
            pltpu.VMEM((2, n) + block, BF16),
            pltpu.VMEM((m, chunks, 2, total, width), BF16),
            pltpu.VMEM((m, total, chans), BF16),
            pltpu.VMEM((2, n) + block, BF16),
            pltpu.VMEM((2, zs * ys) + block, BF16),
            pltpu.VMEM((2, max(zs * (ys - 1), 1)) + block, BF16),
            pltpu.VMEM((2, max(zs - 1, 1)) + block, BF16),
            pltpu.VMEM((2,) + block, BF16),
            pltpu.VMEM((2,) + block, BF16),
            pltpu.VMEM((total + 8, chans), F32),
            pltpu.VMEM((total + 8, lanes), F32),
            pltpu.VMEM((total, chans), F32),
            pltpu.VMEM((total, chans), F32),
            dma(2), dma(4), dma(4),
            dma(2, zs - 1), dma(2, zs * (ys - 1)), dma(2, zs * ys), dma(2, n),
            dma(chunks * (m - 1)), dma(chunks * m), dma(m - 1), dma(m),
            dma(2, zs * ys), dma(2, zs * ys),
            dma(2, zs * (ys - 1)), dma(2, zs * (ys - 1)),
            dma(2, zs - 1), dma(2, zs - 1),
        ],
        compiler_params=pltpu.CompilerParams(
            collective_id=0, has_side_effects=True, vmem_limit_bytes=56 * 2**20
        ),
        cost_estimate=pl.CostEstimate(
            flops=flops, bytes_accessed=12 * 2**20, transcendentals=2 * total * chans
        ),
        name="mixer",
    )(tokens, grad_out, in_weight, conv_weight, conv_bias.reshape(1, chans), out_weight)

    tile = min(depth, 256)
    whole = pl.BlockSpec((total, chans), lambda i: (0, 0))
    strip = pl.BlockSpec((total, tile), lambda i: (0, i))
    fixed = lambda *dims: pl.BlockSpec(dims, lambda i: (0,) * len(dims))
    token = fixed(rows, cols)
    din, dout, out, gtok, tap, bias = pl.pallas_call(
        weight_grads,
        grid=(depth // tile,),
        out_shape=(
            shape(in_weight.shape, F32), shape(out_weight.shape, F32),
            shape((rows, cols), BF16), shape((rows, cols), BF16),
            shape((taps, chans), F32), shape((chans,), F32),
        ),
        in_specs=[
            strip, strip, whole, whole, whole,
            token, token, fixed(taps, chans), fixed(1, chans),
        ],
        out_specs=(
            pl.BlockSpec((2, tile, chans), lambda i: (0, i, 0)),
            pl.BlockSpec((chans, tile), lambda i: (0, i)),
            token, token, fixed(taps, chans), fixed(chans),
        ),
        compiler_params=pltpu.CompilerParams(vmem_limit_bytes=60 * 2**20),
        name="weight_grads",
    )(x, g, hid, gi, gg, out, gtok, tap, bias)
    return (out, gtok, din, dout, tap, bias)


def solution(mesh):
    return jax.shard_map(
        on_device,
        mesh=mesh,
        in_specs=(
            P("seq", "dp"),
            P(None, "seq", "dp"),
            P(None, "dp"),
            P("dp"),
            P("dp", "seq"),
            P("seq", "dp"),
        ),
        out_specs=(
            P("seq", "dp"),
            P("seq", "dp"),
            P(None, "seq", "dp"),
            P("dp", "seq"),
            P(None, "dp"),
            P("dp"),
        ),
        check_vma=False,
    )
```

time: 98 us -> 81.3 us (0.83)
  local copies, waits for them, and re-layouts: 12 us -> 1.26 us
  Pallas kernels: 84.7 us -> 79 us
    unnamed x14 -> x0, local copies, waits for them, and re-layouts: 10.8 us -> none
    pallas_call x1, Pallas kernels: 78 us -> 69.8 us  [on_device(): pl.pallas_call(functools.partial(body, n, m), out_shape=(shape((rows, col...]
    pallas_call x1, Pallas kernels: 6.75 us -> 9.18 us  [on_device(): pl.pallas_call(weight_grads, grid=(depth // tile,), out_shape=(shape(in_w...]
where the time goes in v3:
time: 81.3 us; the launch traced here: 80.9 us
  Pallas kernels  79 us (97%)
  local copies, waits for them, and re-layouts  1.26 us (2%)
    pallas_call x1, Pallas kernels, on_device(): pl.pallas_call(functools.partial(body, n, m), out_shape=(shape((rows, col...  69.8 us
    pallas_call x1, Pallas kernels, on_device(): pl.pallas_call(weight_grads, grid=(depth // tile,), out_shape=(shape(in_w...  9.18 us

profile of v3, /device:TPU:3, one launch (start us, length us, event | category | flops | bytes accessed | tf_op | source)
XLA Modules:
  0.0 80.9 jit_solution(17156440242998606144)
XLA Ops:
  0.6 1.3 %reshape.15.cb_ref = bf16[1,512]{1,0:T(2,128)(2,1)} reshape(bf16[512]{0:T(512)(128)(2,1)} %param.9) | data formatting | bytes 2048 | tf_op jit(solution)/shard_map/reshape | solution.py:386
  1.9 69.8 %mixer.1 = (bf16[128,256]{1,0:T(8,128)(2,1)}, bf16[128,256]{1,0:T(8,128)(2,1)}, bf16[256,2048]{1,0:T(8,128)(2,1)}, bf16[256,2048]{1,0:T(8,128)(2,1)}, bf16[256,5...) custom-call(bf16[128,256]{1,0:T(8,128)(2,1)} %tok.1, ...), custom_call_target="tpu_custom_call" | custom-call | flops 3221225472 | bytes 12582912 | tf_op jit(solution)/shard_map/mixer/pallas_call | solution.py:345
  71.7 9.2 %weight_grads.1 = (f32[2,2048,512]{2,1,0:T(8,128)}, f32[512,2048]{1,0:T(8,128)}, bf16[128,256]{1,0:T(8,128)(2,1)}, bf16[128,256]{1,0:T(8,128)(2,1)}, f32[4,512]{1,0:T(4,128)}, /*index=5*/f32[512]{0:T(512)}) custom-call(bf16[256,2048]{1,0:T(8,128)(2,1)} %get-tuple-element.21.x_ref, bf16[256,2048]{1,0:T(8,128)(2,1)} %get-tuple-element.22.g_ref, ...), custom_call_target="tpu_custom_call" | custom-call | tf_op jit(solution)/shard_map/weight_grads/pallas_call | solution.py:393

commit v4 on v3

--- a/solution.py
+++ b/solution.py
@@ -10,7 +10,6 @@
 F32, BF16 = jnp.float32, jnp.bfloat16
 MESH = pl.DeviceIdType.MESH
 NT = (((1,), (1,)), ((), ()))
-TN = (((0,), (0,)), ((), ()))
 
 
 def silu_parts(value):
@@ -157,12 +156,13 @@
     along_y(1, g_ref)
     for k in range(chunks):
         span = slice(k * width, (k + 1) * width)
-        bslot[seq, :, span] = lax.dot_general(
+        bslot[seq, k] = lax.dot_general(
             g_ref[...], wout[span, :], NT, preferred_element_type=F32
         ).astype(BF16)
-    for d in range(1, m):
-        here = bslot.at[seq]
-        go(here, here, bx_send.at[d - 1], bx_recv.at[seq], {"seq": (seq + d) % m})
+        for d in range(1, m):
+            here = bslot.at[seq, k]
+            go(here, here, bx_send.at[k * (m - 1) + d - 1], bx_recv.at[k * m + seq],
+               {"seq": (seq + d) % m})
 
     def over_seq(read):
         value = read(0).astype(F32)
@@ -173,7 +173,7 @@
     pad[0:8] = jnp.zeros((8, chans), F32)
     pad2[total : total + 8] = jnp.zeros((8, lanes), F32)
     taps_f = cw_ref[...].astype(F32)
-    shift_f = cb_ref[...].astype(F32)
+    shift_f = cb_ref[...].astype(F32).reshape(1, chans)
     for k in range(chunks):
         for d in range(1, m):
             peer = (seq + d) % m
@@ -261,12 +261,15 @@
     to_core(0)
     to_y(0)
 
-    for d in range(1, m):
-        here = bslot.at[(seq + d) % m]
-        send(here, here, bx_send.at[0], bx_recv.at[(seq + d) % m], mate).wait_recv()
     for col in range(0, chans, lanes):
         span = slice(col, col + lanes)
-        back = over_seq(lambda i: bslot[i, :, span])
+        k, local = col // width, slice(col % width, col % width + lanes)
+        if col % width == 0:
+            for d in range(1, m):
+                peer = (seq + d) % m
+                here = bslot.at[peer, k]
+                send(here, here, bx_send.at[0], bx_recv.at[k * m + peer], mate).wait_recv()
+        back = over_seq(lambda i: bslot[i, k, :, local])
         gg_ref[:, span] = (back * sb[:, span]).astype(BF16)
         grad_conv = (back * sa[:, span]).astype(BF16).astype(F32)
         pad2[0:total] = grad_conv
@@ -314,16 +317,20 @@
 
 def weight_grads(
     x_ref, g_ref, hid_ref, gi_ref, gg_ref, out_in, tok_in, tap_in, bias_in,
-    din_ref, dout_ref, out_ref, tok_ref, tap_ref, bias_ref,
+    din_ref, dout_ref, out_ref, tok_ref, tap_ref, bias_ref, turned,
 ):
-    x = x_ref[...]
-    din_ref[0] = lax.dot_general(x, gi_ref[...], TN, preferred_element_type=F32)
-    din_ref[1] = lax.dot_general(x, gg_ref[...], TN, preferred_element_type=F32)
-    dout_ref[...] = lax.dot_general(hid_ref[...], g_ref[...], TN, preferred_element_type=F32)
-    out_ref[...] = out_in[...]
-    tok_ref[...] = tok_in[...]
-    tap_ref[...] = tap_in[...]
-    bias_ref[...] = bias_in[0]
+    @pl.when(pl.program_id(0) == 0)
+    def _():
+        turned[...] = hid_ref[...].T
+        out_ref[...] = out_in[...]
+        tok_ref[...] = tok_in[...]
+        tap_ref[...] = tap_in[...]
+        bias_ref[...] = bias_in[0]
+
+    x = x_ref[...].T
+    din_ref[0] = jnp.dot(x, gi_ref[...], preferred_element_type=F32)
+    din_ref[1] = jnp.dot(x, gg_ref[...], preferred_element_type=F32)
+    dout_ref[...] = jnp.dot(turned[...], g_ref[...], preferred_element_type=F32)
 
 
 def on_device(tokens, in_weight, conv_weight, conv_bias, out_weight, grad_out):
@@ -358,7 +365,7 @@
             pltpu.VMEM(out_weight.shape, BF16),
             pltpu.VMEM((2, n) + block, BF16),
             pltpu.VMEM((m, chunks, 2, total, width), BF16),
-            pltpu.VMEM((m, total, chans), BF16),
+            pltpu.VMEM((m, chunks, total, width), BF16),
             pltpu.VMEM((2, n) + block, BF16),
             pltpu.VMEM((2, zs * ys) + block, BF16),
             pltpu.VMEM((2, max(zs * (ys - 1), 1)) + block, BF16),
@@ -371,7 +378,7 @@
             pltpu.VMEM((total, chans), F32),
             dma(2), dma(4), dma(4),
             dma(2, zs - 1), dma(2, zs * (ys - 1)), dma(2, zs * ys), dma(2, n),
-            dma(chunks * (m - 1)), dma(chunks * m), dma(m - 1), dma(m),
+            dma(chunks * (m - 1)), dma(chunks * m), dma(chunks * (m - 1)), dma(chunks * m),
             dma(2, zs * ys), dma(2, zs * ys),
             dma(2, zs * (ys - 1)), dma(2, zs * (ys - 1)),
             dma(2, zs - 1), dma(2, zs - 1),
@@ -383,7 +390,7 @@
             flops=flops, bytes_accessed=12 * 2**20, transcendentals=2 * total * chans
         ),
         name="mixer",
-    )(tokens, grad_out, in_weight, conv_weight, conv_bias.reshape(1, chans), out_weight)
+    )(tokens, grad_out, in_weight, conv_weight, conv_bias, out_weight)
 
     tile = min(depth, 256)
     whole = pl.BlockSpec((total, chans), lambda i: (0, 0))
@@ -407,6 +414,7 @@
             pl.BlockSpec((chans, tile), lambda i: (0, i)),
             token, token, fixed(taps, chans), fixed(chans),
         ),
+        scratch_shapes=[pltpu.VMEM((chans, total), BF16)],
         compiler_params=pltpu.CompilerParams(vmem_limit_bytes=60 * 2**20),
         name="weight_grads",
     )(x, g, hid, gi, gg, out, gtok, tap, bias)

time: 81.3 us -> 79.8 us (0.982)
  local copies, waits for them, and re-layouts: 1.26 us -> 0 us
    reshape x1 -> x0, local copies, waits for them, and re-layouts: 1.26 us -> none  [on_device(): conv_bias.reshape(1, chans)]
where the time goes in v4:
time: 79.8 us; the launch traced here: 79.5 us
  Pallas kernels  78.8 us (99%)
    pallas_call x1, Pallas kernels, on_device(): pl.pallas_call(functools.partial(body, n, m), out_shape=(shape((rows, col...  69.6 us
    pallas_call x1, Pallas kernels, on_device(): pl.pallas_call(weight_grads, grid=(depth // tile,), out_shape=(shape(in_w...  9.25 us

profile of v4, /device:TPU:3, one launch (start us, length us, event | category | flops | bytes accessed | tf_op | source)
XLA Modules:
  0.0 79.5 jit_solution(15375673932077259068)
XLA Ops:
  0.6 69.6 %mixer.1 = (bf16[128,256]{1,0:T(8,128)(2,1)}, bf16[128,256]{1,0:T(8,128)(2,1)}, bf16[256,2048]{1,0:T(8,128)(2,1)}, bf16[256,2048]{1,0:T(8,128)(2,1)}, bf16[256,5...) custom-call(bf16[128,256]{1,0:T(8,128)(2,1)} %tok.1, ...), custom_call_target="tpu_custom_call" | custom-call | flops 3221225472 | bytes 12582912 | tf_op jit(solution)/shard_map/mixer/pallas_call | solution.py:352
  70.2 9.2 %weight_grads.1 = (f32[2,2048,512]{2,1,0:T(8,128)}, f32[512,2048]{1,0:T(8,128)}, bf16[128,256]{1,0:T(8,128)(2,1)}, bf16[128,256]{1,0:T(8,128)(2,1)}, f32[4,512]{1,0:T(4,128)}, /*index=5*/f32[512]{0:T(512)}) custom-call(bf16[256,2048]{1,0:T(8,128)(2,1)} %get-tuple-element.21.x_ref, bf16[256,2048]{1,0:T(8,128)(2,1)} %get-tuple-element.22.g_ref, ...), custom_call_target="tpu_custom_call" | custom-call | tf_op jit(solution)/shard_map/weight_grads/pallas_call | solution.py:400

commit v5 on v4

--- a/solution.py
+++ b/solution.py
@@ -392,7 +392,7 @@
         name="mixer",
     )(tokens, grad_out, in_weight, conv_weight, conv_bias, out_weight)
 
-    tile = min(depth, 256)
+    tile = min(depth, 512)
     whole = pl.BlockSpec((total, chans), lambda i: (0, 0))
     strip = pl.BlockSpec((total, tile), lambda i: (0, i))
     fixed = lambda *dims: pl.BlockSpec(dims, lambda i: (0,) * len(dims))

time: 79.8 us -> 77.8 us (0.975)
  Pallas kernels: 78.8 us -> 76.9 us
    pallas_call x1, Pallas kernels: 9.25 us -> 7.35 us  [on_device(): pl.pallas_call(weight_grads, grid=(depth // tile,), out_shape=(shape(in_w...]
where the time goes in v5:
time: 77.8 us; the launch traced here: 77.6 us
  Pallas kernels  76.9 us (99%)
    pallas_call x1, Pallas kernels, on_device(): pl.pallas_call(functools.partial(body, n, m), out_shape=(shape((rows, col...  69.6 us
    pallas_call x1, Pallas kernels, on_device(): pl.pallas_call(weight_grads, grid=(depth // tile,), out_shape=(shape(in_w...  7.35 us

profile of v5, /device:TPU:3, one launch (start us, length us, event | category | flops | bytes accessed | tf_op | source)
XLA Modules:
  0.0 77.6 jit_solution(5314096327128668716)
XLA Ops:
  0.6 69.6 %mixer.1 = (bf16[128,256]{1,0:T(8,128)(2,1)}, bf16[128,256]{1,0:T(8,128)(2,1)}, bf16[256,2048]{1,0:T(8,128)(2,1)}, bf16[256,2048]{1,0:T(8,128)(2,1)}, bf16[256,5...) custom-call(bf16[128,256]{1,0:T(8,128)(2,1)} %tok.1, ...), custom_call_target="tpu_custom_call" | custom-call | flops 3221225472 | bytes 12582912 | tf_op jit(solution)/shard_map/mixer/pallas_call | solution.py:352
  70.2 7.3 %weight_grads.1 = (f32[2,2048,512]{2,1,0:T(8,128)}, f32[512,2048]{1,0:T(8,128)}, bf16[128,256]{1,0:T(8,128)(2,1)}, bf16[128,256]{1,0:T(8,128)(2,1)}, f32[4,512]{1,0:T(4,128)}, /*index=5*/f32[512]{0:T(512)}) custom-call(bf16[256,2048]{1,0:T(8,128)(2,1)} %get-tuple-element.21.x_ref, bf16[256,2048]{1,0:T(8,128)(2,1)} %get-tuple-element.22.g_ref, ...), custom_call_target="tpu_custom_call" | custom-call | tf_op jit(solution)/shard_map/weight_grads/pallas_call | solution.py:400
